TPU v7x, 512 devices: a whole 4x8x8 slice. The times are simulated.
512 devices in a mesh: group: 16 (over y, core), owner: 32 (over z, x).
Axes of the slice: x: 4, y: 8, z: 8, core: 2. Of those that a mesh axis runs over, the one named last changes fastest.
Arguments:
- prefix_store: float32 [1024, 16, 128, 128], P(('group', 'owner')), may hold values from -18 to 18
- queries: bfloat16 [65536, 1024], P(('group', 'owner')), may hold values from -6 to 6
- key_rows: bfloat16 [65536, 1024], P(('group', 'owner')), may hold values from -6 to 6
- values: bfloat16 [65536, 2048], P(('group', 'owner')), may hold values from -6 to 6
- log_decay: float32 [65536, 16], P(('group', 'owner')), may hold values from -1 to 0
- write_rate: float32 [65536, 16], P(('group', 'owner')), may hold values from 0.1 to 1
- hit_state: int32 [512], replicated, may hold values from 0 to 1023
- save_slot: int32 [512], replicated, may hold values from 0 to 511, each once
Outputs:
- head_output: bfloat16 [65536, 2048], P(('group', 'owner'))
- checkpoints: float32 [512, 16, 128, 128], P(('group', 'owner'))
Inputs may be any that keep to these rules, and one draw needn't show every extreme that they name: `hit_state`: some stored states are hit by many requests, others by none. `save_slot`: every checkpoint slot is named by exactly one request.
All inputs are finite; a program needn't handle non-finite values.
Results may differ from a plain program's by a relative error of at most 0.001.
Values sent between devices are 32-bit elements; how exact they have to be, the bound alone decides.
A program may use at most 64 MiB of HBM per device.

v0:
```python
import jax
import jax.numpy as jnp
from jax import lax
from jax.sharding import PartitionSpec as P

SPAN = 64


def unit_rows(matrix, head_count, key_dim):
    rows = matrix.astype(jnp.float32).reshape(matrix.shape[0], head_count, key_dim)
    return rows * lax.rsqrt(jnp.sum(rows * rows, axis=-1, keepdims=True) + 1e-06)


def run_blocks(memory, query_hat, key_hat, value_rows, decay_rows, rate_rows, block):
    highest = lax.Precision.HIGHEST
    length = query_hat.shape[0]
    position = jnp.arange(block)
    on_lower = position[:, None] >= position[None, :]
    on_strict = position[:, None] > position[None, :]
    identity = jnp.eye(block, dtype=jnp.float32)
    results = []
    for block_idx in range(length // block):
        first = block_idx * block
        query_blk = query_hat[first : first + block]
        key_blk = key_hat[first : first + block]
        value_blk = value_rows[first : first + block]
        rate_blk = rate_rows[first : first + block].T
        cum_log = jnp.cumsum(decay_rows[first : first + block], axis=0)
        cum_head = cum_log.T
        gap_log = cum_head[:, :, None] - cum_head[:, None, :]
        decay_in = jnp.where(on_lower, jnp.exp(jnp.where(on_lower, gap_log, 0.0)), 0.0)
        key_gram = jnp.einsum("ihd,jhd->hij", key_blk, key_blk, precision=highest)
        amatrix = rate_blk[:, :, None] * key_gram * jnp.where(on_strict, decay_in, 0.0)
        lower_mat = identity[None] + amatrix
        right_mat = identity[None] * rate_blk[:, :, None]
        inverse_t = lax.linalg.triangular_solve(lower_mat, right_mat, left_side=True, lower=True)
        w_keys = jnp.einsum(
            "hij,jhd->hid", inverse_t, key_blk * jnp.exp(cum_log)[:, :, None], precision=highest
        )
        u_values = jnp.einsum("hij,jhe->hie", inverse_t, value_blk, precision=highest)
        new_values = u_values - jnp.einsum("hid,hde->hie", w_keys, memory, precision=highest)
        scores = jnp.einsum("ihd,jhd->hij", query_blk, key_blk, precision=highest) * decay_in
        block_out = jnp.einsum(
            "ihd,hde->ihe", query_blk * jnp.exp(cum_log)[:, :, None], memory, precision=highest
        )
        block_out = block_out + jnp.einsum("hij,hje->ihe", scores, new_values, precision=highest)
        tail_decay = jnp.exp(cum_log[-1])
        weighted_keys = key_blk * jnp.exp(cum_log[-1][None, :] - cum_log)[:, :, None]
        memory = tail_decay[:, None, None] * memory + jnp.einsum(
            "ihd,hie->hde", weighted_keys, new_values, precision=highest
        )
        results.append(block_out)
    return (memory, jnp.concatenate(results, axis=0))


def body(prefix_store, queries, key_rows, values, log_decay, write_rate, hit_state, save_slot):
    groups = lax.axis_size("group")
    owners = lax.axis_size("owner")
    slot_count, head_count, key_dim, value_dim = prefix_store.shape
    piece_rows = head_count * key_dim // (groups * owners)
    length = queries.shape[0]
    key_heads = queries.shape[1] // key_dim
    repeats = head_count // key_heads
    block = min(SPAN, length)
    query_hat = jnp.repeat(
        unit_rows(queries, key_heads, key_dim) * key_dim ** (-0.5), repeats, axis=1
    )
    key_hat = jnp.repeat(unit_rows(key_rows, key_heads, key_dim), repeats, axis=1)
    value_rows = values.astype(jnp.float32).reshape(length, head_count, value_dim)
    laid_store = prefix_store.reshape(1, 1, slot_count, groups, owners, piece_rows, value_dim)
    table = lax.all_to_all(
        lax.all_to_all(laid_store, "group", split_axis=3, concat_axis=0, tiled=True),
        "owner",
        split_axis=4,
        concat_axis=1,
        tiled=True,
    )
    table = table.reshape(groups * owners * slot_count, piece_rows, value_dim)
    wanted = jnp.take(table, hit_state, axis=0).reshape(groups, owners, 1, 1, piece_rows, value_dim)
    fetched = lax.all_to_all(
        lax.all_to_all(wanted, "group", split_axis=0, concat_axis=2, tiled=True),
        "owner",
        split_axis=1,
        concat_axis=3,
        tiled=True,
    )
    start = fetched.reshape(head_count, key_dim, value_dim)
    final_state, outputs = run_blocks(
        start, query_hat, key_hat, value_rows, log_decay, write_rate, block
    )
    head_output = outputs.reshape(length, head_count * value_dim).astype(jnp.bfloat16)
    own_pieces = final_state.reshape(groups, owners, 1, 1, piece_rows, value_dim)
    collected = lax.all_to_all(
        lax.all_to_all(own_pieces, "group", split_axis=0, concat_axis=2, tiled=True),
        "owner",
        split_axis=1,
        concat_axis=3,
        tiled=True,
    )
    collected = collected.reshape(groups * owners, piece_rows, value_dim)
    request_ids = jnp.arange(groups * owners, dtype=jnp.int32)
    sender_of_slot = jnp.zeros((groups * owners,), jnp.int32).at[save_slot].set(request_ids)
    outgoing = jnp.take(collected, sender_of_slot, axis=0).reshape(
        groups, owners, 1, 1, piece_rows, value_dim
    )
    arrived = lax.all_to_all(
        lax.all_to_all(outgoing, "group", split_axis=0, concat_axis=2, tiled=True),
        "owner",
        split_axis=1,
        concat_axis=3,
        tiled=True,
    )
    checkpoints = arrived.reshape(1, head_count, key_dim, value_dim)
    return (head_output, checkpoints)


def solution(mesh):
    in_specs = (
        P(("group", "owner"), None, None, None),
        P(("group", "owner"), None),
        P(("group", "owner"), None),
        P(("group", "owner"), None),
        P(("group", "owner"), None),
        P(("group", "owner"), None),
        P(),
        P(),
    )
    out_specs = (P(("group", "owner"), None), P(("group", "owner"), None, None, None))
    return jax.shard_map(body, mesh=mesh, in_specs=in_specs, out_specs=out_specs, check_vma=False)
```

profile of v0, /device:TPU:1, one launch (start us, length us, event | category | flops | bytes accessed | tf_op | source)
XLA Modules:
  0.0 500.7 jit_solution(2353679501166805829)
XLA Ops:
  0.6 3.2 copy.140
  3.9 60.4 %all_to_all.132 = f32[1,1,2,16,32,4,128]{6,2,4,5,1,0,3:T(2,128)S(1)} all-to-all(f32[1,1,2,16,32,4,128]{6,2,4,5,1,0,3:T(2,128)S(1)} %copy.140), channel_id=1, replica_groups=mesh['group'=16,'owner'=32] {'group'}, dimensions={3} | all-to-all | bytes 4194304 | tf_op jit(solution)/shard_map/all_to_all | solution.py:72
  64.2 2.5 copy.141
  66.8 12.1 %all-to-all-start.1 = ((f32[16,1,2,1,32,4,128]{6,2,0,5,3,1,4:T(2,128)}), f32[16,1,2,1,32,4,128]{6,2,0,5,3,1,4:T(2,128)S(1)}, u32[]{:S(2)}, u32[]{:S(2)}) async-start(f32[16,1,2,1,32,4,128]{6,2,0,5,3,1,4:T(2,128)} %copy.141), calls=%async_computation.1 | async-start | bytes 4194304 | tf_op jit(solution)/shard_map/all_to_all | solution.py:71
  78.9 0.1 copy.183
  79.0 0.2 multiply_reduce_fusion
  79.3 0.2 broadcast_multiply_fusion
  79.5 0.7 fusion.38
  80.4 49.2 %all-to-all-done.1 = f32[16,1,2,1,32,4,128]{6,2,0,5,3,1,4:T(2,128)S(1)} async-done(((f32[16,1,2,1,32,4,128]{6,2,0,5,3,1,4:T(2,128)}), f32[16,1,2,1,32,4,128]{6,2,0,5,3,1,4:T(2,128)S(1)}, u32[]{:S(2)}, u32[]{:S(2)}) %all-to-all-start.1) | async-done | bytes 2097184 | tf_op jit(solution)/shard_map/all_to_all | solution.py:71
  129.5 1.2 copy.142
  130.7 1.4 copy.143
  132.1 2.1 gather_fusion
  134.2 1.5 broadcast_select_fusion.1
  135.7 3.6 all-to-all-start.2
  139.4 0.1 reduce_window_sum.17
  139.7 0.1 reduce_window_sum.18
  140.1 1.8 fusion.7
  141.9 24.6 %all-to-all-done.2 = f32[16,32,1,1,4,128]{5,4,1,3,2,0:T(4,128)S(1)} async-done(((f32[16,32,1,1,4,128]{5,4,1,3,2,0:T(4,128)}), f32[16,32,1,1,4,128]{5,4,1,3,2,0:T(4,128)S(1)}, u32[]{:S(2)}, u32[]{:S(2)}) %all-to-all-start.2) | async-done | bytes 1048608 | tf_op jit(solution)/shard_map/all_to_all | solution.py:81
  166.6 1.3 copy.145
  167.8 5.7 %all-to-all-start.3 = ((f32[1,32,16,1,4,128]{5,4,2,3,0,1:T(4,128)}), f32[1,32,16,1,4,128]{5,4,2,3,0,1:T(4,128)S(1)}, u32[]{:S(2)}, u32[]{:S(2)}) async-start(f32[1,32,16,1,4,128]{5,4,2,3,0,1:T(4,128)} %copy.145), calls=%async_computation.3 | async-start | bytes 2097152 | tf_op jit(solution)/shard_map/all_to_all | solution.py:80
  173.6 1.8 fusion.3
  175.4 79.4 %custom-call.4 = f32[16,1,64,64]{2,3,1,0:T(8,128)S(1)} custom-call(f32[16,1,64,64]{3,2,1,0:T(8,128)} %fusion.7), custom_call_target="InvertDiagBlocksLowerTriangular" | custom-call | tf_op jit(solution)/shard_map/triangular_solve/custom-call.1 | solution.py:36
  254.9 80.0 %custom-call.5 = f32[16,1,64,64]{2,3,1,0:T(8,128)} custom-call(f32[16,1,64,64]{3,2,1,0:T(8,128)} %fusion.3), custom_call_target="InvertDiagBlocksLowerTriangular" | custom-call | tf_op jit(solution)/shard_map/triangular_solve/custom-call.1 | solution.py:36
  335.0 1.1 bitcast_multiply_fusion.3
  336.2 1.1 bitcast_multiply_fusion
  337.4 1.1 fusion.14
  338.5 1.1 fusion.12
  339.7 0.4 fusion.23
  340.1 1.2 fusion.20
  341.3 0.6 fusion.41
  341.9 1.5 fusion.43
  343.4 0.3 copy.146
  343.6 1.1 convolution_subtract_fusion.1
  344.7 1.9 convolution_add_fusion.1
  346.7 1.1 convolution_subtract_fusion
  347.7 1.9 convolution_add_fusion
  349.6 32.2 %all_to_all.133 = f32[16,32,1,1,4,128]{5,4,1,3,2,0:T(4,128)S(1)} all-to-all(f32[16,32,1,1,4,128]{5,4,1,3,2,0:T(4,128)S(1)} %bitcast.149), channel_id=1, replica_groups=mesh['group'=16,'owner'=32] {'group'}, dimensions={0} | all-to-all | bytes 2097152 | tf_op jit(solution)/shard_map/all_to_all | solution.py:94
  381.8 1.3 copy.168
  383.1 9.6 %all-to-all-start.5 = ((f32[1,32,16,1,4,128]{5,4,2,3,0,1:T(4,128)}), f32[1,32,16,1,4,128]{5,4,2,3,0,1:T(4,128)}, u32[]{:S(2)}, u32[]{:S(2)}) async-start(f32[1,32,16,1,4,128]{5,4,2,3,0,1:T(4,128)} %copy.168), calls=%async_computation.5 | async-start | bytes 2097152 | tf_op jit(solution)/shard_map/all_to_all | solution.py:93
  392.7 2.4 scatter_custom_fusion
  395.3 25.1 %all-to-all-done.5 = f32[1,32,16,1,4,128]{5,4,2,3,0,1:T(4,128)} async-done(((f32[1,32,16,1,4,128]{5,4,2,3,0,1:T(4,128)}), f32[1,32,16,1,4,128]{5,4,2,3,0,1:T(4,128)}, u32[]{:S(2)}, u32[]{:S(2)}) %all-to-all-start.5) | async-done | bytes 1048608 | tf_op jit(solution)/shard_map/all_to_all | solution.py:93
  420.3 1.8 copy.169
  422.2 1.6 copy.170
  423.8 3.7 gather_fusion.1
  427.5 2.6 broadcast_select_fusion
  430.1 4.5 all-to-all-start.6
  434.6 0.1 copy.182
  434.7 0.8 copy-done
  435.5 0.2 multiply_reduce_fusion.1
  435.8 26.9 %all-to-all-done.6 = f32[16,32,1,1,4,128]{5,4,1,3,2,0:T(4,128)} async-done(((f32[16,32,1,1,4,128]{5,4,1,3,2,0:T(4,128)}), f32[16,32,1,1,4,128]{5,4,1,3,2,0:T(4,128)}, u32[]{:S(2)}, u32[]{:S(2)}) %all-to-all-start.6) | async-done | bytes 1048608 | tf_op jit(solution)/shard_map/all_to_all | solution.py:107
  462.6 2.5 copy.172
  465.1 5.2 %all-to-all-start.7 = ((f32[1,32,16,1,4,128]{5,4,2,3,0,1:T(4,128)}), f32[1,32,16,1,4,128]{5,4,2,3,0,1:T(4,128)}, u32[]{:S(2)}, u32[]{:S(2)}) async-start(f32[1,32,16,1,4,128]{5,4,2,3,0,1:T(4,128)} %copy.172), calls=%async_computation.7 | async-start | bytes 2097152 | tf_op jit(solution)/shard_map/all_to_all | solution.py:106
  470.4 1.3 multiply_multiply_fusion
  471.9 1.0 convolution_multiply_fusion
  472.9 1.0 convolution_multiply_fusion.2
  473.9 0.6 fusion.44
  474.5 0.6 fusion.42
  475.1 1.1 fusion.10
  476.2 1.1 fusion.11
  477.3 0.3 copy.165
  477.6 1.0 copy.174
  478.6 19.5 %all-to-all-done.7 = f32[1,32,16,1,4,128]{5,4,2,3,0,1:T(4,128)} async-done(((f32[1,32,16,1,4,128]{5,4,2,3,0,1:T(4,128)}), f32[1,32,16,1,4,128]{5,4,2,3,0,1:T(4,128)}, u32[]{:S(2)}, u32[]{:S(2)}) %all-to-all-start.7) | async-done | bytes 1048608 | tf_op jit(solution)/shard_map/all_to_all | solution.py:106
  498.1 1.3 copy.173
  499.5 1.3 copy.175
  (79 shorter events, 1.7 us)
Async XLA Ops:
  66.8 12.1 %copy-start.12 = (bf16[128,1024]{1,0:T(8,128)(2,1)S(1)}, bf16[128,1024]{1,0:T(8,128)(2,1)}, u32[]{:S(2)}) copy-start(bf16[128,1024]{1,0:T(8,128)(2,1)} %param.12) | copy-start | bytes 786436
  66.8 62.8 %all-to-all-start.1 = ((f32[16,1,2,1,32,4,128]{6,2,0,5,3,1,4:T(2,128)}), f32[16,1,2,1,32,4,128]{6,2,0,5,3,1,4:T(2,128)S(1)}, u32[]{:S(2)}, u32[]{:S(2)}) async-start(f32[16,1,2,1,32,4,128]{6,2,0,5,3,1,4:T(2,128)} %copy.141), calls=%async_computation.1 | async-start | bytes 4194304 | tf_op jit(solution)/shard_map/all_to_all | solution.py:71
  78.9 1.4 copy-start.16
  134.2 5.1 %copy-start.14 = (f32[128,16]{0,1:T(8,128)S(1)}, f32[128,16]{0,1:T(8,128)}, u32[]{:S(2)}) copy-start(f32[128,16]{0,1:T(8,128)} %param.14) | copy-start | bytes 24580
  134.2 5.4 %copy-start.9 = (f32[64,8,128]{2,1,0:T(8,128)S(1)}, f32[64,8,128]{2,1,0:T(8,128)}, u32[]{:S(2)}) copy-start(f32[64,8,128]{2,1,0:T(8,128)} %get-tuple-element.18) | copy-start | bytes 786436
  134.2 5.8 %copy-start.15 = (f32[128,16]{0,1:T(8,128)S(1)}, f32[128,16]{0,1:T(8,128)}, u32[]{:S(2)}) copy-start(f32[128,16]{0,1:T(8,128)} %param.15) | copy-start | bytes 24580
  135.7 30.9 %all-to-all-start.2 = ((f32[16,32,1,1,4,128]{5,4,1,3,2,0:T(4,128)}), f32[16,32,1,1,4,128]{5,4,1,3,2,0:T(4,128)S(1)}, u32[]{:S(2)}, u32[]{:S(2)}) async-start(f32[16,32,1,1,4,128]{5,4,1,3,2,0:T(4,128)} %broadcast_select_fusion.1), calls=%async_computation.2 | async-start | bytes 2097152 | tf_op jit(solution)/shard_map/all_to_all | solution.py:81
  140.1 27.8 %copy-start.2 = (f32[64,8,2,128]{3,0,2,1:T(8,128)}, f32[64,8,2,128]{3,0,2,1:T(8,128)S(1)}, u32[]{:S(2)}) copy-start(f32[64,8,2,128]{3,0,2,1:T(8,128)S(1)} %broadcast_in_dim.98) | copy-start | bytes 1572868
  167.8 175.5 %all-to-all-start.3 = ((f32[1,32,16,1,4,128]{5,4,2,3,0,1:T(4,128)}), f32[1,32,16,1,4,128]{5,4,2,3,0,1:T(4,128)S(1)}, u32[]{:S(2)}, u32[]{:S(2)}) async-start(f32[1,32,16,1,4,128]{5,4,2,3,0,1:T(4,128)} %copy.145), calls=%async_computation.3 | async-start | bytes 2097152 | tf_op jit(solution)/shard_map/all_to_all | solution.py:80
  173.6 163.7 %copy-start.4 = (f32[64,8,2,128]{3,0,2,1:T(8,128)}, f32[64,8,2,128]{3,0,2,1:T(8,128)S(1)}, u32[]{:S(2)}) copy-start(f32[64,8,2,128]{3,0,2,1:T(8,128)S(1)} %broadcast_in_dim.103) | copy-start | bytes 1572868
  173.6 163.7 %copy-start.10 = (bf16[128,2048]{1,0:T(8,128)(2,1)S(1)}, bf16[128,2048]{1,0:T(8,128)(2,1)}, u32[]{:S(2)}) copy-start(bf16[128,2048]{1,0:T(8,128)(2,1)} %param.13) | copy-start | bytes 1572868
  335.0 3.5 copy-start.11
  343.4 1.4 copy-start.8
  344.7 1.9 copy-start.1
  344.7 1.9 copy-start.6
  346.7 1.1 copy-start.7
  381.8 10.9 %copy-start.17 = (s32[512]{0:T(512)S(1)}, s32[512]{0:T(512)}, u32[]{:S(2)}) copy-start(s32[512]{0:T(512)} %param.17) | copy-start | bytes 6148
  383.1 37.3 %all-to-all-start.5 = ((f32[1,32,16,1,4,128]{5,4,2,3,0,1:T(4,128)}), f32[1,32,16,1,4,128]{5,4,2,3,0,1:T(4,128)}, u32[]{:S(2)}, u32[]{:S(2)}) async-start(f32[1,32,16,1,4,128]{5,4,2,3,0,1:T(4,128)} %copy.168), calls=%async_computation.5 | async-start | bytes 2097152 | tf_op jit(solution)/shard_map/all_to_all | solution.py:93
  427.5 7.0 %copy-start.13 = (bf16[128,1024]{1,0:T(8,128)(2,1)S(1)}, bf16[128,1024]{1,0:T(8,128)(2,1)}, u32[]{:S(2)}) copy-start(bf16[128,1024]{1,0:T(8,128)(2,1)} %param.11) | copy-start | bytes 786436
  430.1 32.6 %all-to-all-start.6 = ((f32[16,32,1,1,4,128]{5,4,1,3,2,0:T(4,128)}), f32[16,32,1,1,4,128]{5,4,1,3,2,0:T(4,128)}, u32[]{:S(2)}, u32[]{:S(2)}) async-start(f32[16,32,1,1,4,128]{5,4,1,3,2,0:T(4,128)} %broadcast_select_fusion), calls=%async_computation.6 | async-start | bytes 2097152 | tf_op jit(solution)/shard_map/all_to_all | solution.py:107
  434.7 0.8 copy-start
  465.1 33.0 %all-to-all-start.7 = ((f32[1,32,16,1,4,128]{5,4,2,3,0,1:T(4,128)}), f32[1,32,16,1,4,128]{5,4,2,3,0,1:T(4,128)}, u32[]{:S(2)}, u32[]{:S(2)}) async-start(f32[1,32,16,1,4,128]{5,4,2,3,0,1:T(4,128)} %copy.172), calls=%async_computation.7 | async-start | bytes 2097152 | tf_op jit(solution)/shard_map/all_to_all | solution.py:106
  470.4 1.5 copy-start.5
  471.7 1.2 copy-start.3
where the time goes:
time: 502 us; the launch traced here: 501 us
  other arithmetic  168 us (33%)
  waiting for transfers between devices  145 us (29%)
  blocking collectives  92.5 us (18%)
  starting transfers between devices  40.6 us (8%)
  local copies, waits for them, and re-layouts  32.3 us (6%)
  matrix products  20.6 us (4%)
    another operation x3, other arithmetic, run_blocks(): lax.linalg.triangular_solve(lower_mat, right_mat, left_side=True, lower=T...  159 us
    all_to_all x1, blocking collectives, body(): lax.all_to_all(laid_store, 'group', split_axis=3, concat_axis=0, tiled=True)  60.4 us
    all_to_all x1, waiting for transfers between devices, body(): lax.all_to_all(lax.all_to_all(laid_store, 'group', split_axis=3, concat_a...  49.2 us
    all_to_all x1, blocking collectives, body(): lax.all_to_all(own_pieces, 'group', split_axis=0, concat_axis=2, tiled=True)  32.2 us
    all_to_all x1, waiting for transfers between devices, body(): lax.all_to_all(outgoing, 'group', split_axis=0, concat_axis=2, tiled=True)  26.9 us
    all_to_all x1, waiting for transfers between devices, body(): lax.all_to_all(lax.all_to_all(own_pieces, 'group', split_axis=0, concat_a...  25.1 us
    all_to_all x1, waiting for transfers between devices, body(): lax.all_to_all(wanted, 'group', split_axis=0, concat_axis=2, tiled=True)  24.6 us
    all_to_all x1, waiting for transfers between devices, body(): lax.all_to_all(lax.all_to_all(outgoing, 'group', split_axis=0, concat_axi...  19.5 us
  transfers between devices with their start and end apart: 6, of which 5 were waited for; matrix products, arithmetic and copies ran while one was open for 37% of the time, Pallas kernels for 0%

commit v1 on v0

v1 whole, which is shorter than its diff:
```python
import functools

import jax
import jax.numpy as jnp
from jax import lax
from jax.experimental import pallas as pl
from jax.experimental.pallas import tpu as pltpu
from jax.sharding import PartitionSpec as P

SPAN = 64
F32 = jnp.float32
BF16 = jnp.bfloat16


def split(x):
    hi = x.astype(BF16)
    return hi, (x - hi.astype(F32)).astype(BF16)


def wide(x):
    return jnp.concatenate(split(x), axis=1)


def fold(x):
    half = x.shape[1] // 2
    return x[:, :half] + x[:, half:]


def dot(a, b):
    return lax.dot_general(a, b, (((1,), (0,)), ((), ())), preferred_element_type=F32)


def dot_exact(a, b):
    return fold(dot(a, wide(b)))


def dot_pair(a_wide, b):
    both = wide(b)
    return fold(dot(a_wide, jnp.concatenate([both, both], axis=0)))


def dot_full(a, b):
    return dot_pair(wide(a), b)


def iota(shape, dim):
    return lax.broadcasted_iota(jnp.int32, shape, dim)


def pick(mask, x, axis):
    return jnp.sum(jnp.where(mask, x, jnp.zeros_like(x)), axis=axis, keepdims=True)


class Plan:
    def __init__(self, first, second, n_first, n_second):
        self.axes = (first, second)
        self.sizes = (n_first, n_second)


def kernel(
    groups, owners, chunks, heads, key_heads, length,
    store, q, k, v, ld, wr, hit, slot,
    out, ckpt,
    r1, t1, r2, w3, r3, t3, r4, fin, r5, t5, r6, w7, r7, t7,
    m1, m2, inv, sco, cum_ref, cumt_ref,
    send_sem, recv_sem, own_sem,
):
    total = groups * owners
    me = {"group": lax.axis_index("group"), "owner": lax.axis_index("owner")}
    count = {"group": groups, "owner": owners}
    per_chunk = heads // chunks
    repeat = heads // key_heads

    def route(chunk):
        return ("group", "owner") if chunk % 2 == 0 else ("owner", "group")

    def turn(axis, step):
        odd = step % 2
        n = count[axis]
        offset = (1 - odd) * (step // 2 + 1) + odd * (n - (step + 1) // 2)
        return (me[axis] + offset) % n

    barrier = pltpu.get_barrier_semaphore()
    for axis in ("group", "owner"):
        def greet(step, carry, axis=axis):
            pl.semaphore_signal(
                barrier, inc=1, device_id={axis: turn(axis, step)},
                device_id_type=pl.DeviceIdType.MESH,
            )
            return carry
        lax.fori_loop(0, count[axis] - 1, greet, 0)
    pl.semaphore_wait(barrier, groups + owners - 2)

    def remote(axis, src, dst, chunk, stage, target):
        return pltpu.make_async_remote_copy(
            src_ref=src, dst_ref=dst,
            send_sem=send_sem.at[chunk, stage], recv_sem=recv_sem.at[chunk, stage],
            device_id={axis: target}, device_id_type=pl.DeviceIdType.MESH,
        )

    def send(chunk, stage, axis, src, dst, rows):
        def go(step, carry):
            target = turn(axis, step)
            remote(
                axis,
                src.at[chunk, pl.ds(pl.multiple_of(target * rows, 8), rows)],
                dst.at[chunk, pl.ds(pl.multiple_of(me[axis] * rows, 8), rows)],
                chunk, stage, target,
            ).start()
            return carry
        lax.fori_loop(0, count[axis] - 1, go, 0)

    def keep(chunk, axis, src, dst, rows):
        place = pl.ds(pl.multiple_of(me[axis] * rows, 8), rows)
        dst[chunk, place] = src[chunk, place]

    def await_recv(chunk, stage, axis, dst, rows):
        part = dst.at[chunk, pl.ds(0, (count[axis] - 1) * rows)]
        remote(axis, part, part, chunk, stage, turn(axis, 0)).wait_recv()

    def await_send(chunk, stage, axis, src, rows):
        part = src.at[chunk, pl.ds(0, (count[axis] - 1) * rows)]
        remote(axis, part, part, chunk, stage, turn(axis, 0)).wait_send()

    def regroup(chunk, src, dst, n_outer, n_inner):
        for inner in range(n_inner):
            dst[chunk, pl.ds(inner * n_outer, n_outer), :] = src[
                chunk, pl.ds(inner, n_outer, stride=n_inner), :
            ]

    def select(chunk, matrix, src, dst):
        rows = src.shape[1]
        both = wide(src[chunk])
        strip = 128
        for first in range(0, total, strip):
            dst[chunk, pl.ds(first, strip), :] = fold(
                dot(matrix[chunk % 2, pl.ds(first, strip), :], both)
            )

    def stage1(chunk):
        axis, other = route(chunk)
        rows = count[other]

        def go(step, carry):
            target = turn(axis, step)
            for state in range(2):
                remote(
                    axis,
                    store.at[state, chunk, pl.ds(pl.multiple_of(target * rows, 8), rows)],
                    r1.at[chunk, pl.ds(pl.multiple_of((me[axis] * 2 + state) * rows, 8), rows)],
                    chunk, 0, target,
                ).start()
            return carry
        lax.fori_loop(0, count[axis] - 1, go, 0)
        for state in range(2):
            pltpu.make_async_copy(
                store.at[state, chunk, pl.ds(pl.multiple_of(me[axis] * rows, 8), rows)],
                r1.at[chunk, pl.ds(pl.multiple_of((me[axis] * 2 + state) * rows, 8), rows)],
                own_sem.at[chunk, state],
            ).start()

    def stage2(chunk):
        axis, other = route(chunk)
        rows = count[other]
        for state in range(2):
            pltpu.make_async_copy(
                store.at[state, chunk, pl.ds(pl.multiple_of(me[axis] * rows, 8), rows)],
                r1.at[chunk, pl.ds(pl.multiple_of((me[axis] * 2 + state) * rows, 8), rows)],
                own_sem.at[chunk, state],
            ).wait()
        await_recv(chunk, 0, axis, r1, 2 * rows)
        regroup(chunk, r1, t1, 2 * count[axis], rows)
        send(chunk, 1, other, t1, r2, 2 * count[axis])
        keep(chunk, other, t1, r2, 2 * count[axis])

    def stage3(chunk):
        axis, other = route(chunk)
        await_recv(chunk, 1, other, r2, 2 * count[axis])
        select(chunk, m1, r2, w3)
        send(chunk, 2, other, w3, r3, count[axis])
        keep(chunk, other, w3, r3, count[axis])

    def stage4(chunk):
        axis, other = route(chunk)
        await_recv(chunk, 2, other, r3, count[axis])
        regroup(chunk, r3, t3, count[other], count[axis])
        send(chunk, 3, axis, t3, r4, count[other])
        keep(chunk, axis, t3, r4, count[other])

    def stage5(chunk):
        axis, other = route(chunk)
        await_recv(chunk, 3, axis, r4, count[other])
        advance(chunk)
        send(chunk, 4, axis, fin, r5, count[other])
        keep(chunk, axis, fin, r5, count[other])

    def stage6(chunk):
        axis, other = route(chunk)
        await_recv(chunk, 4, axis, r5, count[other])
        regroup(chunk, r5, t5, count[axis], count[other])
        send(chunk, 5, other, t5, r6, count[axis])
        keep(chunk, other, t5, r6, count[axis])

    def stage7(chunk):
        axis, other = route(chunk)
        await_recv(chunk, 5, other, r6, count[axis])
        select(chunk, m2, r6, w7)
        send(chunk, 6, other, w7, r7, count[axis])
        keep(chunk, other, w7, r7, count[axis])

    def stage8(chunk):
        axis, other = route(chunk)
        await_recv(chunk, 6, other, r7, count[axis])
        regroup(chunk, r7, t7, count[other], count[axis])
        send(chunk, 7, axis, t7, ckpt, count[other])
        keep(chunk, axis, t7, ckpt, count[other])

    def stage9(chunk):
        axis, other = route(chunk)
        await_recv(chunk, 7, axis, ckpt, count[other])

    def index_matrices():
        strip = 128
        hit_row, slot_row = hit[...], slot[...]

        def swap(x):
            return (x % groups) * owners + x // groups

        slot_swapped = jnp.zeros((1, total), jnp.int32)
        for first in range(0, total, strip):
            place = pl.ds(first, strip)
            row = iota((strip, total), 0) + first
            lane = iota((strip, total), 1)
            hit_natural = pick(row == lane, hit_row, 1)
            hit_swapped = pick(swap(row) == lane, hit_row, 1)
            slot_natural = pick(row == lane, slot_row, 1)
            slot_swapped = slot_swapped + pick(row == swap(lane), slot_natural, 0)
            state = iota((strip, 2 * total), 1)
            named = ((state // 2) % groups * owners + state // (2 * groups)) * 2 + state % 2
            one = jnp.ones((), F32)
            zero = jnp.zeros((), F32)
            m1[0, place, :] = jnp.where(hit_swapped == named, one, zero).astype(BF16)
            m1[1, place, :] = jnp.where(hit_natural == state, one, zero).astype(BF16)
            m2[1, place, :] = jnp.where(slot_row == row, one, zero).astype(BF16)
        for first in range(0, total, strip):
            row = iota((strip, total), 0) + first
            m2[0, pl.ds(first, strip), :] = jnp.where(
                slot_swapped == swap(row), one, zero
            ).astype(BF16)

    square = (length, length)

    def same(size):
        return iota(square, 0) // size == iota(square, 1) // size

    def cumulate():
        lower = (iota(square, 0) >= iota(square, 1)) & same(SPAN)
        ones = jnp.where(lower, jnp.ones((), F32), jnp.zeros((), F32))
        cum = jnp.dot(
            ones, ld[...], precision=lax.Precision.HIGHEST, preferred_element_type=F32
        )
        cum_ref[...] = cum
        padded = jnp.concatenate([cum, jnp.zeros((length, length - heads), F32)], axis=1)
        cumt_ref[...] = padded.T[:heads]

    def prepare(chunk, carry):
        row, col = iota(square, 0), iota(square, 1)
        eye = row == col
        lower = (row >= col) & same(SPAN)
        strict = (row > col) & same(SPAN)
        unit = jnp.where(eye, jnp.ones((), F32), jnp.zeros((), F32))
        lane = iota((length, heads), 1)
        key_dim = q.shape[1] // key_heads
        amats = []
        for inner in range(per_chunk // repeat):
            key_head = chunk * (per_chunk // repeat) + inner
            place = pl.ds(pl.multiple_of(key_head * key_dim, 128), key_dim)
            key, query = k[:, place], q[:, place]
            trans = (((1,), (1,)), ((), ()))
            gram = lax.dot_general(key, key, trans, preferred_element_type=F32)
            cross = lax.dot_general(query, key, trans, preferred_element_type=F32)
            key_col = lax.rsqrt(pick(eye, gram, 1) + 1e-06)
            key_row = lax.rsqrt(pick(eye, gram, 0) + 1e-06)
            query32 = query.astype(F32)
            query_col = lax.rsqrt(
                jnp.sum(query32 * query32, axis=1, keepdims=True) + 1e-06
            ) * key_dim ** (-0.5)
            gram = gram * key_col * key_row
            cross = cross * query_col * key_row
            for extra in range(repeat):
                head = key_head * repeat + extra
                cum_col = pick(lane == head, cum_ref[...], 1)
                rate_col = pick(lane == head, wr[...], 1)
                gap = cum_col - cumt_ref[pl.ds(head, 1), :]
                decay = jnp.where(lower, jnp.exp(jnp.where(lower, gap, 0.0)), 0.0)
                sco[head] = wide(cross * decay)
                amats.append((head, jnp.where(strict, rate_col * gram * decay, 0.0)))
        results = []
        small = 8
        within = same(small)
        diag = [jnp.where(within, a, 0.0) for _, a in amats]
        xs = [unit - b for b in diag]
        for _ in range(2):
            diag = [dot_full(b, b) for b in diag]
            xs = [x + dot_full(x, b) for x, b in zip(xs, diag)]
        size = small
        while size < SPAN:
            cross_mask = same(2 * size) & ~same(size)
            parts = [jnp.where(cross_mask, a, 0.0) for _, a in amats]
            inner_products = [dot_full(p, x) for p, x in zip(parts, xs)]
            xs = [x - dot_full(x, p) for x, p in zip(xs, inner_products)]
            size *= 2
        for (head, _), x in zip(amats, xs):
            inv[head] = wide(x)
        return carry

    def advance(chunk):
        key_dim = q.shape[1] // key_heads
        value_dim = v.shape[1] // heads
        head_list = [chunk * per_chunk + i for i in range(per_chunk)]
        states = [r4[chunk, pl.ds(i * key_dim, key_dim), :] for i in range(per_chunk)]
        for first in range(0, length, SPAN):
            rows = pl.ds(first, SPAN)
            block = (first, first + SPAN)
            reads, scales = [], []
            for i, head in enumerate(head_list):
                cols = pl.ds(head // repeat * key_dim, key_dim)
                both = jnp.concatenate([k[rows, cols], q[rows, cols]], axis=0)
                reads.append(dot_exact(both, states[i]))
            news = []
            for i, head in enumerate(head_list):
                cols = pl.ds(head // repeat * key_dim, key_dim)
                key32 = k[rows, cols].astype(F32)
                query32 = q[rows, cols].astype(F32)
                key_scale = lax.rsqrt(jnp.sum(key32 * key32, axis=1, keepdims=True) + 1e-06)
                query_scale = lax.rsqrt(
                    jnp.sum(query32 * query32, axis=1, keepdims=True) + 1e-06
                ) * key_dim ** (-0.5)
                cum_col = cum_ref[rows, head : head + 1]
                last = cum_ref[pl.ds(first + SPAN - 1, 1), head : head + 1]
                grown = jnp.exp(cum_col)
                rate = wr[rows, head : head + 1]
                value = v[rows, pl.ds(head * value_dim, value_dim)].astype(F32)
                rest = rate * (value - (grown * key_scale) * reads[i][:SPAN])
                matrix = inv[head, rows, :]
                left = jnp.concatenate(
                    [matrix[:, first : first + SPAN],
                     matrix[:, length + first : length + first + SPAN]], axis=1
                )
                news.append(dot_pair(left, rest))
                scales.append((query_scale * grown, key_scale * jnp.exp(last - cum_col), jnp.exp(last)))
            for i, head in enumerate(head_list):
                cols = pl.ds(head // repeat * key_dim, key_dim)
                query_scale, key_scale, tail = scales[i]
                matrix = sco[head, rows, :]
                left = jnp.concatenate(
                    [matrix[:, first : first + SPAN],
                     matrix[:, length + first : length + first + SPAN]], axis=1
                )
                result = query_scale * reads[i][SPAN:] + dot_pair(left, news[i])
                out[rows, pl.ds(head * value_dim, value_dim)] = result.astype(out.dtype)
                key_t = k[rows, cols].T
                states[i] = tail * states[i] + dot_exact(key_t, key_scale * news[i])
        for i in range(per_chunk):
            fin[chunk, pl.ds(i * key_dim, key_dim), :] = states[i]

    stage1(0)
    stage1(1)
    index_matrices()
    cumulate()
    lax.fori_loop(0, chunks, prepare, 0)
    stage1(2)
    stage1(3)
    ahead, behind = (0, 1), (2, 3)
    lead = [stage2, stage3, stage4, stage5, stage6, stage7, stage8, stage9]
    for step in range(len(lead) + 1):
        if step < len(lead):
            for chunk in ahead:
                lead[step](chunk)
        if step >= 1:
            for chunk in behind:
                lead[step - 1](chunk)
    for chunk in range(chunks):
        axis, other = route(chunk)
        na, nb = count[axis], count[other]
        await_send(chunk, 0, axis, r1, 2 * nb)
        await_send(chunk, 1, other, t1, 2 * na)
        await_send(chunk, 2, other, w3, na)
        await_send(chunk, 3, axis, t3, nb)
        await_send(chunk, 4, axis, fin, nb)
        await_send(chunk, 5, other, t5, na)
        await_send(chunk, 6, other, w7, na)
        await_send(chunk, 7, axis, t7, nb)


def body(prefix_store, queries, key_rows, values, log_decay, write_rate, hit_state, save_slot):
    groups = lax.axis_size("group")
    owners = lax.axis_size("owner")
    slots, heads, key_dim, value_dim = prefix_store.shape
    total = groups * owners
    length = queries.shape[0]
    key_heads = queries.shape[1] // key_dim
    chunks = heads * key_dim // total
    vmem = pl.BlockSpec(memory_space=pltpu.VMEM)
    anywhere = pl.BlockSpec(memory_space=pl.ANY)
    one = pltpu.VMEM((chunks, total, value_dim), F32)
    two = pltpu.VMEM((chunks, 2 * total, value_dim), F32)
    head_output, checkpoints = pl.pallas_call(
        functools.partial(kernel, groups, owners, chunks, heads, key_heads, length),
        out_shape=(
            jax.ShapeDtypeStruct((length, heads * value_dim), BF16),
            jax.ShapeDtypeStruct((chunks, total, value_dim), F32),
        ),
        in_specs=[anywhere] + [vmem] * 7,
        out_specs=(vmem, vmem),
        scratch_shapes=[
            two, two, two, one, one, one, one, one, one, one, one, one, one, one,
            pltpu.VMEM((2, total, 2 * total), BF16),
            pltpu.VMEM((2, total, total), BF16),
            pltpu.VMEM((heads, length, 2 * length), BF16),
            pltpu.VMEM((heads, length, 2 * length), BF16),
            pltpu.VMEM((length, heads), F32),
            pltpu.VMEM((heads, length), F32),
            pltpu.SemaphoreType.DMA((chunks, 8)),
            pltpu.SemaphoreType.DMA((chunks, 8)),
            pltpu.SemaphoreType.DMA((chunks, 2)),
        ],
        compiler_params=pltpu.CompilerParams(
            collective_id=0, has_side_effects=True, vmem_limit_bytes=56 * 1024 * 1024
        ),
        cost_estimate=pl.CostEstimate(
            flops=4 * 10**9, bytes_accessed=6 * 2**20, transcendentals=2**19
        ),
    )(
        prefix_store.reshape(slots, chunks, total, value_dim),
        queries, key_rows, values, log_decay, write_rate,
        hit_state.reshape(1, total), save_slot.reshape(1, total),
    )
    return head_output, checkpoints.reshape(1, heads, key_dim, value_dim)


def solution(mesh):
    split_rows = P(("group", "owner"), None)
    split_states = P(("group", "owner"), None, None, None)
    in_specs = (split_states,) + (split_rows,) * 5 + (P(), P())
    return jax.shard_map(
        body, mesh=mesh, in_specs=in_specs, out_specs=(split_rows, split_states), check_vma=False
    )
```

time: 502 us -> 157 us (0.31)
  other arithmetic: 168 us -> 0 us
  Pallas kernels: 0 us -> 147 us
  waiting for transfers between devices: 145 us -> 0 us
  blocking collectives: 92.5 us -> 0 us
  starting transfers between devices: 40.6 us -> 0 us
  local copies, waits for them, and re-layouts: 32.3 us -> 7.03 us
  matrix products: 20.6 us -> 0 us
    another operation x5 -> x0, other arithmetic: 160 us -> none  [the longest x3 159 us: run_blocks(): lax.linalg.triangular_solve(lower_mat, right_mat, left_side=True, lower=T...]
    pallas_call x0 -> x1, Pallas kernels: none -> 147 us  [body(): pl.pallas_call(functools.partial(kernel, groups, owners, chunks, heads, k...]
    all_to_all x6 -> x0, waiting for transfers between devices: 145 us -> none  [the longest x1 49.2 us: body(): lax.all_to_all(lax.all_to_all(laid_store, 'group', split_axis=3, concat_a...]
    all_to_all x2 -> x0, blocking collectives: 92.5 us -> none  [the longest x1 60.4 us: body(): lax.all_to_all(laid_store, 'group', split_axis=3, concat_axis=0, tiled=True)]
    all_to_all x6 -> x0, starting transfers between devices: 40.6 us -> none  [the longest x1 12.1 us: body(): lax.all_to_all(lax.all_to_all(laid_store, 'group', split_axis=3, concat_a...]
    dot_general x16 -> x0, matrix products: 18.3 us -> none  [the longest x2 3.76 us: run_blocks(): jnp.einsum('ihd,hie->hde', weighted_keys, new_values, precision=highest)]
    all_to_all x8 -> x0, local copies, waits for them, and re-layouts: 12.1 us -> none  [the longest x1 2.53 us: body(): lax.all_to_all(laid_store, 'group', split_axis=3, concat_axis=0, tiled=True)]
    reshape x3 -> x0, local copies, waits for them, and re-layouts: 6.22 us -> none  [the longest x1 3.23 us: body(): prefix_store.reshape(1, 1, slot_count, groups, owners, piece_rows, value_...]
  transfers between devices with their start and end apart: 6 -> 0, of which waited for: 5 -> 0; matrix products, arithmetic and copies ran while one was open for 37% -> 0% of each run, Pallas kernels for 0% -> 0%
where the time goes in v1:
time: 157 us; the launch traced here: 154 us
  Pallas kernels  147 us (94%)
  local copies, waits for them, and re-layouts  7.03 us (4%)
    pallas_call x1, Pallas kernels, body(): pl.pallas_call(functools.partial(kernel, groups, owners, chunks, heads, k...  147 us
    unnamed x4, local copies, waits for them, and re-layouts  7.03 us

profile of v1, /device:TPU:1, one launch (start us, length us, event | category | flops | bytes accessed | tf_op | source)
XLA Modules:
  0.0 154.2 jit_solution(10296432035505420902)
XLA Ops:
  0.6 1.4 copy.10.ld
  2.1 1.4 copy.11.wr
  3.5 146.5 %shard_map.95 = (bf16[128,2048]{1,0:T(8,128)(2,1)}, f32[4,512,128]{2,1,0:T(8,128)}) custom-call(f32[2,4,512,128]{3,2,1,0:T(8,128)} %bitcast.5, bf16[128,1024]{1,0:T(8,128)(2,1)} %q.1, bf16[128,1024]{1,0:T(8,128)(2,1)} %k.1, bf16[128,2048]{1,0:T(8,128)(2,1)} %v.1, f32[128,16]{1,0:T(8,128)} %copy.10.ld, f32[128,16]{1,0:T(8,128)} %copy.11.wr, ...), custom_call_target="tpu_custom_call" | custom-call | flops 4000000000 | bytes 6291456 | tf_op jit(solution)/shard_map/pallas_call | solution.py:408
  150.0 1.9 %copy.14 = bf16[128,2048]{1,0:T(8,128)(2,1)} copy(bf16[128,2048]{1,0:T(8,128)(2,1)} %get-tuple-element.8) | data formatting | bytes 1048576
  151.9 2.3 %copy.15 = f32[1,16,128,128]{3,2,1,0:T(8,128)} copy(f32[1,16,128,128]{3,2,1,0:T(8,128)} %bitcast.4) | data formatting | bytes 2097152

commit v2 on v1

--- a/solution.py
+++ b/solution.py
@@ -51,20 +51,25 @@
     return jnp.sum(jnp.where(mask, x, jnp.zeros_like(x)), axis=axis, keepdims=True)
 
 
-class Plan:
-    def __init__(self, first, second, n_first, n_second):
-        self.axes = (first, second)
-        self.sizes = (n_first, n_second)
+LOW = {"group": 2, "owner": 4}
+CELL, PLANE = 11, 48
 
 
 def kernel(
-    groups, owners, chunks, heads, key_heads, length,
+    packed, groups, owners, chunks, heads, key_heads, length,
     store, q, k, v, ld, wr, hit, slot,
-    out, ckpt,
-    r1, t1, r2, w3, r3, t3, r4, fin, r5, t5, r6, w7, r7, t7,
-    m1, m2, inv, sco, cum_ref, cumt_ref,
-    send_sem, recv_sem, own_sem,
+    *refs,
 ):
+    if packed:
+        out, ckpt, flag, *refs = refs
+        sv, s0, r0, t0, hc, mk, mf, *refs = refs
+    else:
+        out, ckpt, *refs = refs
+    (
+        r1, t1, r2, w3, r3, t3, r4, fin, r5, t5, r6, w7, r7, t7,
+        m1, m2, inv, sco, cum_ref, cumt_ref, rate_ref,
+        send_sem, recv_sem, own_sem,
+    ) = refs
     total = groups * owners
     me = {"group": lax.axis_index("group"), "owner": lax.axis_index("owner")}
     count = {"group": groups, "owner": owners}
@@ -74,11 +79,38 @@
     def route(chunk):
         return ("group", "owner") if chunk % 2 == 0 else ("owner", "group")
 
+    low = {axis: me[axis] % LOW[axis] for axis in me}
+    high = {axis: me[axis] // LOW[axis] for axis in me}
+    highs = {axis: count[axis] // LOW[axis] for axis in me}
+    cell = LOW["group"] * LOW["owner"]
+    place_in_cell = low["owner"] * LOW["group"] + low["group"]
+
+    def shift(step, n):
+        odd = step % 2
+        return (1 - odd) * (step // 2 + 1) + odd * (n - (step + 1) // 2)
+
     def turn(axis, step):
-        odd = step % 2
-        n = count[axis]
-        offset = (1 - odd) * (step // 2 + 1) + odd * (n - (step + 1) // 2)
-        return (me[axis] + offset) % n
+        n, part = count[axis], LOW[axis]
+        offset = shift(step, n)
+        inner = (low[axis] + offset % part) % part
+        outer = (high[axis] + offset // part) % (n // part)
+        return outer * part + inner
+
+    def turn_high(axis, step):
+        return (high[axis] + shift(step, highs[axis])) % highs[axis]
+
+    def cell_target(index):
+        return {
+            "group": high["group"] * LOW["group"] + index % LOW["group"],
+            "owner": high["owner"] * LOW["owner"] + index // LOW["group"],
+        }
+
+    if packed:
+        for chunk in range(chunks):
+            for state in range(2):
+                pltpu.make_async_copy(
+                    store.at[state, chunk], sv.at[chunk, state], own_sem.at[chunk, state]
+                ).start()
 
     barrier = pltpu.get_barrier_semaphore()
     for axis in ("group", "owner"):
@@ -89,7 +121,18 @@
             )
             return carry
         lax.fori_loop(0, count[axis] - 1, greet, 0)
-    pl.semaphore_wait(barrier, groups + owners - 2)
+    greeted = groups + owners - 2
+    if packed:
+        def greet_cell(step, carry):
+            inner = (low["owner"] + step + 1) % LOW["owner"]
+            pl.semaphore_signal(
+                barrier, inc=1,
+                device_id=cell_target(inner * LOW["group"] + 1 - low["group"]),
+                device_id_type=pl.DeviceIdType.MESH,
+            )
+            return carry
+        lax.fori_loop(0, LOW["owner"] - 1, greet_cell, 0)
+        greeted = greeted + LOW["owner"] - 1
 
     def remote(axis, src, dst, chunk, stage, target):
         return pltpu.make_async_remote_copy(
@@ -136,6 +179,100 @@
             dst[chunk, pl.ds(first, strip), :] = fold(
                 dot(matrix[chunk % 2, pl.ds(first, strip), :], both)
             )
+
+    def send_high(chunk, stage, axis, src, dst, rows):
+        def go(step, carry):
+            target = turn_high(axis, step)
+            remote(
+                axis,
+                src.at[chunk, pl.ds(pl.multiple_of(target * rows, 8), rows)],
+                dst.at[chunk, pl.ds(pl.multiple_of(high[axis] * rows, 8), rows)],
+                chunk, stage, target * LOW[axis] + low[axis],
+            ).start()
+            return carry
+        lax.fori_loop(0, highs[axis] - 1, go, 0)
+        mine = pl.ds(pl.multiple_of(high[axis] * rows, 8), rows)
+        dst[chunk, mine] = src[chunk, mine]
+
+    def await_high(chunk, stage, axis, dst, rows):
+        part = dst.at[chunk, pl.ds(0, (highs[axis] - 1) * rows)]
+        copy = remote(axis, part, part, chunk, stage, turn(axis, 0))
+        return copy
+
+    def cell_copy(chunk, target):
+        rows = 2 * highs["group"] * highs["owner"]
+        return pltpu.make_async_remote_copy(
+            src_ref=s0.at[chunk, pl.ds(pl.multiple_of(target * rows, 8), rows)],
+            dst_ref=r0.at[chunk, pl.ds(pl.multiple_of(place_in_cell * rows, 8), rows)],
+            send_sem=send_sem.at[chunk, 8], recv_sem=recv_sem.at[chunk, 8],
+            device_id=cell_target(target), device_id_type=pl.DeviceIdType.MESH,
+        )
+
+    def await_cell(chunk, ref):
+        rows = 2 * highs["group"] * highs["owner"]
+        part = ref.at[chunk, pl.ds(0, (cell - 1) * rows)]
+        return pltpu.make_async_remote_copy(
+            src_ref=part, dst_ref=part,
+            send_sem=send_sem.at[chunk, 8], recv_sem=recv_sem.at[chunk, 8],
+            device_id=cell_target((place_in_cell + 1) % cell),
+            device_id_type=pl.DeviceIdType.MESH,
+        )
+
+    def packed0(chunk):
+        axis, other = route(chunk)
+        n_outer, n_inner = highs[axis], highs[other]
+        rows = n_outer * n_inner
+        for state in range(2):
+            pltpu.make_async_copy(
+                store.at[state, chunk], sv.at[chunk, state], own_sem.at[chunk, state]
+            ).wait()
+        for index in range(cell):
+            inner = {"group": index % LOW["group"], "owner": index // LOW["group"]}
+            for state in range(2):
+                for outer in range(n_outer):
+                    first = (outer * LOW[axis] + inner[axis]) * count[other] + inner[other]
+                    s0[chunk, pl.ds((index * 2 + state) * rows + outer * n_inner, n_inner), :] = sv[
+                        chunk, state, pl.ds(first, n_inner, stride=LOW[other]), :
+                    ]
+
+    def packed_start(chunk):
+        rows = highs["group"] * highs["owner"]
+
+        def go(step, carry):
+            cell_copy(chunk, (place_in_cell + shift(step, cell)) % cell).start()
+            return carry
+        lax.fori_loop(0, cell - 1, go, 0)
+        mine = pl.ds(pl.multiple_of(place_in_cell * 2 * rows, 8), 2 * rows)
+        r0[chunk, mine] = s0[chunk, mine]
+
+    def packed1(chunk):
+        axis, other = route(chunk)
+        n_outer, n_inner = highs[axis], highs[other]
+        rows = n_outer * n_inner
+        await_cell(chunk, r0).wait_recv()
+        for outer in range(n_outer):
+            held = jnp.concatenate(
+                [r0[chunk, pl.ds(i * rows + outer * n_inner, n_inner), :] for i in range(2 * cell)],
+                axis=0,
+            )
+            t0[chunk, pl.ds(outer * CELL * n_inner, CELL * n_inner), :] = dot_exact(mk[...], held)
+        send_high(chunk, 0, axis, t0, r1, CELL * n_inner)
+
+    def packed2(chunk):
+        axis, other = route(chunk)
+        n_outer, n_inner = highs[axis], highs[other]
+        await_high(chunk, 0, axis, r1, CELL * n_inner).wait_recv()
+        for inner in range(n_inner):
+            held = r1[chunk, pl.ds(inner, n_outer * CELL, stride=n_inner), :]
+            t1[chunk, pl.ds(inner * PLANE, PLANE), :] = dot_exact(mf[chunk % 2], held)
+        send_high(chunk, 1, other, t1, r2, PLANE)
+
+    def packed3(chunk):
+        axis, other = route(chunk)
+        await_high(chunk, 1, other, r2, PLANE).wait_recv()
+        select(chunk, m1, r2, w3)
+        send(chunk, 2, other, w3, r3, count[axis])
+        keep(chunk, other, w3, r3, count[axis])
 
     def stage1(chunk):
         axis, other = route(chunk)
@@ -248,20 +385,141 @@
                 slot_swapped == swap(row), one, zero
             ).astype(BF16)
 
+    def packed_matrices():
+        strip = 128
+        n_y, n_z = highs["group"], highs["owner"]
+        held = 2 * cell
+        lanes = n_z * held
+        one = jnp.ones((), F32)
+        zero = jnp.zeros((), F32)
+
+        def mark(mask):
+            return jnp.where(mask, one, zero)
+
+        def swap(x):
+            return (x % groups) * owners + x // groups
+
+        hit_row, slot_row = hit[...], slot[...]
+        slot_swapped = jnp.zeros((1, total), jnp.int32)
+        for first in range(0, total, strip):
+            place = pl.ds(first, strip)
+            row = iota((strip, total), 0) + first
+            lane = iota((strip, total), 1)
+            spread = (strip, lanes)
+            hc[0, place, :] = jnp.broadcast_to(pick(swap(row) == lane, hit_row, 1), spread)
+            hc[1, place, :] = jnp.broadcast_to(pick(row == lane, hit_row, 1), spread)
+            slot_natural = pick(row == lane, slot_row, 1)
+            slot_swapped = slot_swapped + pick(row == swap(lane), slot_natural, 0)
+            m2[1, place, :] = mark(slot_row == row).astype(BF16)
+        for first in range(0, total, strip):
+            row = iota((strip, total), 0) + first
+            m2[0, pl.ds(first, strip), :] = mark(slot_swapped == swap(row)).astype(BF16)
+
+        lane = iota((1, lanes), 1)
+        in_cell = lane % held
+        owner_of = lane // held * LOW["owner"] + in_cell // (2 * LOW["group"])
+        core_of = in_cell // 2 % LOW["group"]
+        names = [
+            ((y * LOW["group"] + core_of) * owners + owner_of) * 2 + lane % 2 for y in range(n_y)
+        ]
+        present = jnp.concatenate(
+            [jnp.max(mark(hc[1] == name), axis=0, keepdims=True) for name in names], axis=0
+        )
+        a, b = iota((lanes, lanes), 0), iota((lanes, lanes), 1)
+        here = present.astype(BF16)
+        rank = dot(here, mark((a // held == b // held) & (a < b)).astype(BF16))
+        number = dot(here, mark(a // held == b // held).astype(BF16))
+        before_z = dot(here, mark(a // held < b // held).astype(BF16))
+        running = jnp.zeros((1, lanes), F32)
+        before = []
+        for y in range(n_y):
+            before.append(running)
+            running = running + number[y : y + 1]
+        before_y = jnp.concatenate(before, axis=0)
+        own_row = iota((n_y, lanes), 0)
+        z_of = (iota((n_y, lanes), 1) // held).astype(F32)
+        place_in = (
+            z_of * PLANE + before_y + rank,
+            own_row.astype(F32) * PLANE + before_z + rank,
+        )
+        excess = jnp.maximum(
+            jnp.max(number - CELL, axis=(0, 1), keepdims=True),
+            jnp.maximum(
+                jnp.max(running - PLANE, axis=(0, 1), keepdims=True),
+                jnp.max(before_z + number - PLANE, axis=(0, 1), keepdims=True),
+            ),
+        )
+        flag[0, 0] = jnp.max(excess)
+
+        for way, n_parts in ((0, n_z), (1, n_y)):
+            for first in range(0, total, strip):
+                rows = pl.ds(first, strip)
+                wanted = hc[way, rows, :]
+                found = jnp.zeros((strip, lanes), F32)
+                for y, name in enumerate(names):
+                    found = found + jnp.where(wanted == name, place_in[way][y : y + 1], zero)
+                found = jnp.sum(found, axis=1, keepdims=True)
+                table = iota((strip, n_parts * PLANE), 1).astype(F32)
+                m1[way, rows, :] = mark(found == table).astype(BF16)
+
+        n_inner = lanes // held
+        mine = pick(own_row == high["group"], present * (rank + one), 0)
+        a, b = iota((lanes, held * n_inner), 0), iota((lanes, held * n_inner), 1)
+        own_cell = (a // held == high["owner"]) & (a % held == b // n_inner)
+        entry = dot(
+            jnp.broadcast_to(mine, (8, lanes)).astype(BF16), mark(own_cell).astype(BF16)
+        )[:1]
+        shape = (CELL * n_inner, held * n_inner)
+        row, col = iota(shape, 0), iota(shape, 1)
+        mk[...] = mark(
+            (entry == (row // n_inner + 1).astype(F32)) & (row % n_inner == col % n_inner)
+        ).astype(BF16)
+
+        def fill(way, base, amount, n_parts):
+            shape = (PLANE, n_parts * CELL)
+            row = iota(shape, 0).astype(F32)
+            nth = (iota((1, n_parts * CELL), 1) % CELL).astype(F32)
+            mf[way] = mark((base + nth == row) & (nth < amount)).astype(BF16)
+
+        own_lane = iota((n_y, lanes), 1) == high["owner"] * held
+        sub, lane = iota((n_y, n_y * CELL), 0), iota((n_y, n_y * CELL), 1)
+        spread_y = [
+            pick(sub == lane // CELL, jnp.broadcast_to(pick(own_lane, x, 1), sub.shape), 0)
+            for x in (before_y, number)
+        ]
+        fill(0, *spread_y, n_y)
+        a, b = iota((lanes, n_z * CELL), 0), iota((lanes, n_z * CELL), 1)
+        expand = mark(a == b // CELL * held).astype(BF16)
+        spread_z = [
+            dot(
+                jnp.broadcast_to(
+                    pick(own_row == high["group"], x, 0), (8, lanes)
+                ).astype(BF16),
+                expand,
+            )[:1]
+            for x in (before_z, number)
+        ]
+        fill(1, *spread_z, n_z)
+
     square = (length, length)
 
     def same(size):
         return iota(square, 0) // size == iota(square, 1) // size
+
+    def turned(x):
+        padded = jnp.concatenate([x, jnp.zeros((length - heads, length), F32)], axis=0)
+        return padded.T[:, :heads]
 
     def cumulate():
         lower = (iota(square, 0) >= iota(square, 1)) & same(SPAN)
         ones = jnp.where(lower, jnp.ones((), F32), jnp.zeros((), F32))
         cum = jnp.dot(
-            ones, ld[...], precision=lax.Precision.HIGHEST, preferred_element_type=F32
+            ones, turned(ld[...]), precision=lax.Precision.HIGHEST, preferred_element_type=F32
         )
         cum_ref[...] = cum
         padded = jnp.concatenate([cum, jnp.zeros((length, length - heads), F32)], axis=1)
         cumt_ref[...] = padded.T[:heads]
+        rate_ref[...] = turned(wr[...])
 
     def prepare(chunk, carry):
         row, col = iota(square, 0), iota(square, 1)
@@ -290,7 +548,7 @@
             for extra in range(repeat):
                 head = key_head * repeat + extra
                 cum_col = pick(lane == head, cum_ref[...], 1)
-                rate_col = pick(lane == head, wr[...], 1)
+                rate_col = pick(lane == head, rate_ref[...], 1)
                 gap = cum_col - cumt_ref[pl.ds(head, 1), :]
                 decay = jnp.where(lower, jnp.exp(jnp.where(lower, gap, 0.0)), 0.0)
                 sco[head] = wide(cross * decay)
@@ -339,7 +597,7 @@
                 cum_col = cum_ref[rows, head : head + 1]
                 last = cum_ref[pl.ds(first + SPAN - 1, 1), head : head + 1]
                 grown = jnp.exp(cum_col)
-                rate = wr[rows, head : head + 1]
+                rate = rate_ref[rows, head : head + 1]
                 value = v[rows, pl.ds(head * value_dim, value_dim)].astype(F32)
                 rest = rate * (value - (grown * key_scale) * reads[i][:SPAN])
                 matrix = inv[head, rows, :]
@@ -364,27 +622,54 @@
         for i in range(per_chunk):
             fin[chunk, pl.ds(i * key_dim, key_dim), :] = states[i]
 
-    stage1(0)
-    stage1(1)
-    index_matrices()
-    cumulate()
-    lax.fori_loop(0, chunks, prepare, 0)
-    stage1(2)
-    stage1(3)
+    if packed:
+        for chunk in range(chunks):
+            packed0(chunk)
+        packed_matrices()
+        cumulate()
+        pl.semaphore_wait(barrier, greeted)
+        for chunk in range(chunks):
+            packed_start(chunk)
+        prepare(0, 0)
+        packed1(0)
+        packed1(1)
+        prepare(1, 0)
+        lead = [packed2, packed3]
+    else:
+        pl.semaphore_wait(barrier, greeted)
+        stage1(0)
+        stage1(1)
+        index_matrices()
+        cumulate()
+        lax.fori_loop(0, chunks, prepare, 0)
+        stage1(2)
+        stage1(3)
+        lead = [stage2, stage3]
+    lead = lead + [stage4, stage5, stage6, stage7, stage8, stage9]
     ahead, behind = (0, 1), (2, 3)
-    lead = [stage2, stage3, stage4, stage5, stage6, stage7, stage8, stage9]
     for step in range(len(lead) + 1):
         if step < len(lead):
             for chunk in ahead:
                 lead[step](chunk)
+        if step == 0 and packed:
+            for chunk in behind:
+                packed1(chunk)
+            prepare(2, 0)
+        if step == 1 and packed:
+            prepare(3, 0)
         if step >= 1:
             for chunk in behind:
                 lead[step - 1](chunk)
     for chunk in range(chunks):
         axis, other = route(chunk)
         na, nb = count[axis], count[other]
-        await_send(chunk, 0, axis, r1, 2 * nb)
-        await_send(chunk, 1, other, t1, 2 * na)
+        if packed:
+            await_cell(chunk, s0).wait_send()
+            await_high(chunk, 0, axis, t0, CELL * highs[other]).wait_send()
+            await_high(chunk, 1, other, t1, PLANE).wait_send()
+        else:
+            await_send(chunk, 0, axis, r1, 2 * nb)
+            await_send(chunk, 1, other, t1, 2 * na)
         await_send(chunk, 2, other, w3, na)
         await_send(chunk, 3, axis, t3, nb)
         await_send(chunk, 4, axis, fin, nb)
@@ -393,7 +678,7 @@
         await_send(chunk, 7, axis, t7, nb)
 
 
-def body(prefix_store, queries, key_rows, values, log_decay, write_rate, hit_state, save_slot):
+def run(packed, prefix_store, queries, key_rows, values, log_decay, write_rate, hit_state, save_slot):
     groups = lax.axis_size("group")
     owners = lax.axis_size("owner")
     slots, heads, key_dim, value_dim = prefix_store.shape
@@ -403,40 +688,74 @@
     chunks = heads * key_dim // total
     vmem = pl.BlockSpec(memory_space=pltpu.VMEM)
     anywhere = pl.BlockSpec(memory_space=pl.ANY)
-    one = pltpu.VMEM((chunks, total, value_dim), F32)
-    two = pltpu.VMEM((chunks, 2 * total, value_dim), F32)
-    head_output, checkpoints = pl.pallas_call(
-        functools.partial(kernel, groups, owners, chunks, heads, key_heads, length),
-        out_shape=(
-            jax.ShapeDtypeStruct((length, heads * value_dim), BF16),
-            jax.ShapeDtypeStruct((chunks, total, value_dim), F32),
-        ),
+
+    def buffer(rows):
+        return pltpu.VMEM((chunks, rows, value_dim), F32)
+
+    out_shape = [
+        jax.ShapeDtypeStruct((length, heads * value_dim), BF16),
+        jax.ShapeDtypeStruct((chunks, total, value_dim), F32),
+    ]
+    out_specs = [vmem, vmem]
+    scratch = []
+    if packed:
+        cell = LOW["group"] * LOW["owner"]
+        n_y, n_z = groups // LOW["group"], owners // LOW["owner"]
+        assert n_y == n_z == 8 and cell == 8 and n_z * 2 * cell == 128
+        out_shape.append(jax.ShapeDtypeStruct((1, 1), F32))
+        out_specs.append(pl.BlockSpec(memory_space=pltpu.SMEM))
+        scratch = [
+            pltpu.VMEM((chunks, 2, total, value_dim), F32),
+            buffer(2 * total), buffer(2 * total), buffer(n_y * n_z * CELL),
+            pltpu.VMEM((2, total, 128), jnp.int32),
+            pltpu.VMEM((CELL * n_z, 2 * cell * n_z), BF16),
+            pltpu.VMEM((2, PLANE, n_y * CELL), BF16),
+        ]
+        spread = [n_y * n_z * CELL, n_z * PLANE, n_z * PLANE]
+    else:
+        spread = [2 * total] * 3
+    results = pl.pallas_call(
+        functools.partial(kernel, packed, groups, owners, chunks, heads, key_heads, length),
+        out_shape=out_shape,
         in_specs=[anywhere] + [vmem] * 7,
-        out_specs=(vmem, vmem),
-        scratch_shapes=[
-            two, two, two, one, one, one, one, one, one, one, one, one, one, one,
-            pltpu.VMEM((2, total, 2 * total), BF16),
+        out_specs=out_specs,
+        scratch_shapes=scratch + [buffer(rows) for rows in spread] + [buffer(total)] * 11 + [
+            pltpu.VMEM((2, total, spread[2]), BF16),
             pltpu.VMEM((2, total, total), BF16),
             pltpu.VMEM((heads, length, 2 * length), BF16),
             pltpu.VMEM((heads, length, 2 * length), BF16),
             pltpu.VMEM((length, heads), F32),
             pltpu.VMEM((heads, length), F32),
-            pltpu.SemaphoreType.DMA((chunks, 8)),
-            pltpu.SemaphoreType.DMA((chunks, 8)),
+            pltpu.VMEM((length, heads), F32),
+            pltpu.SemaphoreType.DMA((chunks, 9)),
+            pltpu.SemaphoreType.DMA((chunks, 9)),
             pltpu.SemaphoreType.DMA((chunks, 2)),
         ],
         compiler_params=pltpu.CompilerParams(
-            collective_id=0, has_side_effects=True, vmem_limit_bytes=56 * 1024 * 1024
+            collective_id=0 if packed else 1, has_side_effects=True,
+            vmem_limit_bytes=56 * 1024 * 1024,
         ),
         cost_estimate=pl.CostEstimate(
             flops=4 * 10**9, bytes_accessed=6 * 2**20, transcendentals=2**19
         ),
     )(
         prefix_store.reshape(slots, chunks, total, value_dim),
-        queries, key_rows, values, log_decay, write_rate,
+        queries, key_rows, values, log_decay.T, write_rate.T,
         hit_state.reshape(1, total), save_slot.reshape(1, total),
     )
-    return head_output, checkpoints.reshape(1, heads, key_dim, value_dim)
+    results = list(results)
+    results[1] = results[1].reshape(1, heads, key_dim, value_dim)
+    return results
+
+
+def body(*args):
+    head_output, checkpoints, excess = run(True, *args)
+    return lax.cond(
+        excess[0, 0] > 0,
+        lambda operands, done: tuple(run(False, *operands)),
+        lambda operands, done: done,
+        args, (head_output, checkpoints),
+    )
 
 
 def solution(mesh):

time: 157 us -> 144 us (0.917); the launches traced: 154 us -> 144 us
  Pallas kernels: 147 us -> 141 us
  local copies, waits for them, and re-layouts: 7.03 us -> 1.79 us
    pallas_call x1, Pallas kernels: 147 us -> 141 us  [run(): pl.pallas_call(functools.partial(kernel, packed, groups, owners, chunks,...]
    unnamed x4 -> x16, local copies, waits for them, and re-layouts: 7.03 us -> 1.79 us
where the time goes in v2:
time: 144 us
  Pallas kernels  141 us (98%)
  local copies, waits for them, and re-layouts  1.79 us (1%)
    pallas_call x1, Pallas kernels, run(): pl.pallas_call(functools.partial(kernel, packed, groups, owners, chunks,...  141 us

profile of v2, /device:TPU:1, one launch (start us, length us, event | category | flops | bytes accessed | tf_op | source)
XLA Modules:
  0.0 143.7 jit_solution(8679542953427788989)
XLA Ops:
  0.6 0.0 copy-start
  0.6 0.0 copy-start.1
  0.7 0.0 copy-start.2
  0.7 0.0 copy-start.3
  0.7 0.0 copy-start.4
  0.7 0.0 copy-start.5
  0.7 0.0 copy-start.6
  0.7 140.5 %shard_map.95 = (bf16[128,2048]{1,0:T(8,128)(2,1)S(1)}, f32[4,512,128]{2,1,0:T(8,128)S(1)}, f32[1,1]{1,0:T(1,128)}) custom-call(f32[2,4,512,128]{3,2,1,0:T(8,128)} %bitcast.13, bf16[128,1024]{1,0:T(8,128)(2,1)} %q.1, bf16[128,1024]{1,0:T(8,128)(2,1)} %k.1, bf16[128,2048]{1,0:T(8,128)(2,1)} %v.1, f32[16,128]{1,0:T(8,128)} %bitcast.15, f32[16,128]{1,0:T(8,128)} %bitcast.17, ...), custom_call_target="tpu_custom_call" | custom-call | flops 4000000000 | bytes 6291456 | tf_op jit(solution)/shard_map/pallas_call | solution.py:717
  141.9 0.0 copy-done
  141.9 0.0 copy-done.1
  141.9 0.0 copy-done.2
  141.9 0.0 copy-done.3
  141.9 0.0 copy-done.4
  141.9 0.0 copy-done.5
  141.9 0.0 copy-done.6
  142.0 0.8 copy.16
  142.8 1.0 copy.17
  (1 shorter events, 0.0 us)
Async XLA Ops:
  0.6 141.3 %copy-start = (bf16[128,2048]{1,0:T(8,128)(2,1)S(1)}, bf16[128,2048]{1,0:T(8,128)(2,1)}, u32[]{:S(2)}) copy-start(bf16[128,2048]{1,0:T(8,128)(2,1)} %v.1) | copy-start | bytes 1572868
  0.6 141.3 %copy-start.1 = (bf16[128,1024]{1,0:T(8,128)(2,1)S(1)}, bf16[128,1024]{1,0:T(8,128)(2,1)}, u32[]{:S(2)}) copy-start(bf16[128,1024]{1,0:T(8,128)(2,1)} %q.1) | copy-start | bytes 786436
  0.7 141.3 %copy-start.2 = (bf16[128,1024]{1,0:T(8,128)(2,1)S(1)}, bf16[128,1024]{1,0:T(8,128)(2,1)}, u32[]{:S(2)}) copy-start(bf16[128,1024]{1,0:T(8,128)(2,1)} %k.1) | copy-start | bytes 786436
  0.7 141.3 %copy-start.3 = (f32[128,16]{0,1:T(8,128)S(1)}, f32[128,16]{0,1:T(8,128)}, u32[]{:S(2)}) copy-start(f32[128,16]{0,1:T(8,128)} %param.14) | copy-start | bytes 24580
  0.7 141.3 %copy-start.4 = (f32[128,16]{0,1:T(8,128)S(1)}, f32[128,16]{0,1:T(8,128)}, u32[]{:S(2)}) copy-start(f32[128,16]{0,1:T(8,128)} %param.15) | copy-start | bytes 24580
  0.7 141.3 %copy-start.5 = (s32[512]{0:T(512)S(1)}, s32[512]{0:T(512)}, u32[]{:S(2)}) copy-start(s32[512]{0:T(512)} %param.16) | copy-start | bytes 6148
  0.7 141.3 %copy-start.6 = (s32[512]{0:T(512)S(1)}, s32[512]{0:T(512)}, u32[]{:S(2)}) copy-start(s32[512]{0:T(512)} %param.17) | copy-start | bytes 6148

commit v3 on v2

--- a/solution.py
+++ b/solution.py
@@ -646,20 +646,15 @@
         stage1(3)
         lead = [stage2, stage3]
     lead = lead + [stage4, stage5, stage6, stage7, stage8, stage9]
-    ahead, behind = (0, 1), (2, 3)
-    for step in range(len(lead) + 1):
-        if step < len(lead):
-            for chunk in ahead:
-                lead[step](chunk)
-        if step == 0 and packed:
-            for chunk in behind:
-                packed1(chunk)
+    for step, stage in enumerate(lead):
+        if packed and step == 0:
+            packed1(2)
+            packed1(3)
             prepare(2, 0)
-        if step == 1 and packed:
+        if packed and step == 1:
             prepare(3, 0)
-        if step >= 1:
-            for chunk in behind:
-                lead[step - 1](chunk)
+        for chunk in range(chunks):
+            stage(chunk)
     for chunk in range(chunks):
         axis, other = route(chunk)
         na, nb = count[axis], count[other]

time: 144 us -> 139 us (0.965)
  Pallas kernels: 141 us -> 134 us
    pallas_call x1, Pallas kernels: 141 us -> 134 us  [run(): pl.pallas_call(functools.partial(kernel, packed, groups, owners, chunks,...]
where the time goes in v3:
time: 139 us; the launch traced here: 138 us
  Pallas kernels  134 us (96%)
  local copies, waits for them, and re-layouts  1.79 us (1%)
    pallas_call x1, Pallas kernels, run(): pl.pallas_call(functools.partial(kernel, packed, groups, owners, chunks,...  134 us

profile of v3, /device:TPU:1, one launch (start us, length us, event | category | flops | bytes accessed | tf_op | source)
XLA Modules:
  0.0 137.6 jit_solution(17088873155843479415)
XLA Ops:
  0.6 0.0 copy-start
  0.6 0.0 copy-start.1
  0.7 0.0 copy-start.2
  0.7 0.0 copy-start.3
  0.7 0.0 copy-start.4
  0.7 0.0 copy-start.5
  0.7 0.0 copy-start.6
  0.7 134.4 %shard_map.95 = (bf16[128,2048]{1,0:T(8,128)(2,1)S(1)}, f32[4,512,128]{2,1,0:T(8,128)S(1)}, f32[1,1]{1,0:T(1,128)}) custom-call(f32[2,4,512,128]{3,2,1,0:T(8,128)} %bitcast.13, bf16[128,1024]{1,0:T(8,128)(2,1)} %q.1, bf16[128,1024]{1,0:T(8,128)(2,1)} %k.1, bf16[128,2048]{1,0:T(8,128)(2,1)} %v.1, f32[16,128]{1,0:T(8,128)} %bitcast.15, f32[16,128]{1,0:T(8,128)} %bitcast.17, ...), custom_call_target="tpu_custom_call" | custom-call | flops 4000000000 | bytes 6291456 | tf_op jit(solution)/shard_map/pallas_call | solution.py:712
  135.7 0.0 copy-done
  135.7 0.0 copy-done.1
  135.8 0.0 copy-done.2
  135.8 0.0 copy-done.3
  135.8 0.0 copy-done.4
  135.8 0.0 copy-done.5
  135.8 0.0 copy-done.6
  135.8 0.8 copy.16
  136.6 1.0 copy.17
  (1 shorter events, 0.0 us)
Async XLA Ops:
  0.6 135.1 %copy-start = (bf16[128,2048]{1,0:T(8,128)(2,1)S(1)}, bf16[128,2048]{1,0:T(8,128)(2,1)}, u32[]{:S(2)}) copy-start(bf16[128,2048]{1,0:T(8,128)(2,1)} %v.1) | copy-start | bytes 1572868
  0.6 135.1 %copy-start.1 = (bf16[128,1024]{1,0:T(8,128)(2,1)S(1)}, bf16[128,1024]{1,0:T(8,128)(2,1)}, u32[]{:S(2)}) copy-start(bf16[128,1024]{1,0:T(8,128)(2,1)} %q.1) | copy-start | bytes 786436
  0.7 135.1 %copy-start.2 = (bf16[128,1024]{1,0:T(8,128)(2,1)S(1)}, bf16[128,1024]{1,0:T(8,128)(2,1)}, u32[]{:S(2)}) copy-start(bf16[128,1024]{1,0:T(8,128)(2,1)} %k.1) | copy-start | bytes 786436
  0.7 135.1 %copy-start.3 = (f32[128,16]{0,1:T(8,128)S(1)}, f32[128,16]{0,1:T(8,128)}, u32[]{:S(2)}) copy-start(f32[128,16]{0,1:T(8,128)} %param.14) | copy-start | bytes 24580
  0.7 135.1 %copy-start.4 = (f32[128,16]{0,1:T(8,128)S(1)}, f32[128,16]{0,1:T(8,128)}, u32[]{:S(2)}) copy-start(f32[128,16]{0,1:T(8,128)} %param.15) | copy-start | bytes 24580
  0.7 135.1 %copy-start.5 = (s32[512]{0:T(512)S(1)}, s32[512]{0:T(512)}, u32[]{:S(2)}) copy-start(s32[512]{0:T(512)} %param.16) | copy-start | bytes 6148
  0.7 135.1 %copy-start.6 = (s32[512]{0:T(512)S(1)}, s32[512]{0:T(512)}, u32[]{:S(2)}) copy-start(s32[512]{0:T(512)} %param.17) | copy-start | bytes 6148
